TPU v7x, 512 devices: a whole 4x8x8 slice. The times are simulated.
512 devices in a mesh: inst: 8 (over z_hi, x), space: 64 (over z_lo, y, core).
Axes of the slice: x: 4, y: 8, z: 8 (z_hi: 2, z_lo: 4; z = z_hi * 4 + z_lo), core: 2. Of those that a mesh axis runs over, the one named last changes fastest.
Arguments:
- objective_grad: float32 [16, 5, 131072], P('inst', None, 'space'), may hold values from -6 to 6
- face_jacobians: bfloat16 [16, 6, 5, 5, 131072], P('inst', None, None, None, 'space'), may hold values from -0.75 to 0.75
- plane_jacobians: bfloat16 [16, 5, 5, 8192], P('inst', None, None, 'space'), may hold values from -2 to 2
- diagonal_inverse: float32 [16, 5, 5, 131072], P('inst', None, None, 'space'), as said below
- neighbours: int32 [6, 131072], P(None, 'space'), may hold values from 0 to 2303, as said below
- plane_source: int32 [64], P('space'), may hold values from 0 to 63, each once
Outputs:
- adjoint: float32 [16, 5, 131072], P('inst', None, 'space')
Inputs may be any that keep to these rules, and one draw needn't show every extreme that they name: `neighbours`: every neighbour index lies within one block row of 128 cells of the cell itself: from i % 2048 to i % 2048 + 256. `plane_source`: each index appears once. `diagonal_inverse`: each 5x5 block has its diagonal between 0.5 and 1.1 and off-diagonal entries of size up to about 0.5.
All inputs are finite; a program needn't handle non-finite values.
Results may differ from a plain program's by a relative error of at most 0.0003.
Values sent between devices are 32-bit elements; how exact they have to be, the bound alone decides.
A program may use at most 64 MiB of HBM per device.

v0:
```python
import math

import jax
import jax.numpy as jnp
from jax import lax
from jax.sharding import PartitionSpec as P

ITERS = 2


frequency = 0.05


def padded_2(shard, sides, width):
    for axis, dim in sides:
        devices, length = (lax.axis_size(axis), shard.shape[dim])
        up = [(i, (i + 1) % devices) for i in range(devices)]
        down = [(j, i) for i, j in up]
        last = lax.slice_in_dim(shard, length - width, length, axis=dim)
        first = lax.slice_in_dim(shard, 0, width, axis=dim)
        before = lax.ppermute(last, axis, up)
        after = lax.ppermute(first, axis, down)
        shard = jnp.concatenate([before, shard, after], axis=dim)
    return shard


def spectral_matrix(count):
    rows = jnp.arange(count)[:, None]
    cols = jnp.arange(count)[None, :]
    diff = (rows - cols).astype(jnp.float32)
    parity = 1.0 - 2.0 * jnp.mod(rows - cols, 2).astype(jnp.float32)
    same = rows == cols
    safe = jnp.where(same, 1.0, jnp.tan(math.pi * diff / count))
    return jnp.where(same, 0.0, 0.5 * parity / safe)


def apply_inverse(inverse, values):
    return jnp.sum(inverse * values[:, :, None, :], axis=1)


def face_sum(padded, face_jacobians, neighbours, summed):
    inst_local = padded.shape[0]
    comps = padded.shape[1]
    face_count = neighbours.shape[0]
    block_count = summed.shape[2] // 128
    window_pos = jnp.arange(384, dtype=jnp.int32)

    def one_block(block, total):
        start = (block * 128).astype(jnp.int32)
        window = lax.dynamic_slice_in_dim(padded, start, 384, 2).reshape(inst_local * comps, 384)
        local_idx = lax.dynamic_slice_in_dim(neighbours, start, 128, 1) - start
        onehot = (window_pos[None, :, None] == local_idx[:, None, :]).astype(jnp.float32)
        beside = jnp.einsum("rw,kwc->rkc", window, onehot, precision=lax.Precision.HIGHEST)
        beside = beside.reshape(inst_local, comps, face_count, 128)
        jac_block = lax.dynamic_slice_in_dim(face_jacobians, start, 128, 4).astype(jnp.float32)
        part_sum = jnp.einsum("nkabc,nakc->nbc", jac_block, beside, precision=lax.Precision.HIGHEST)
        return lax.dynamic_update_slice_in_dim(total, part_sum, start, 2)

    return lax.fori_loop(0, block_count, one_block, summed)


def body(
    objective_grad, face_jacobians, plane_jacobians, diagonal_inverse, neighbours, plane_source
):
    inst_local = objective_grad.shape[0]
    total_inst = inst_local * lax.axis_size("inst")
    first_inst = lax.axis_index("inst") * inst_local
    coupling = spectral_matrix(total_inst)
    own_cols = lax.dynamic_slice_in_dim(coupling, first_inst, inst_local, 1)
    adjoint = apply_inverse(diagonal_inverse, objective_grad)
    for sweep_no in range(ITERS):
        padded = padded_2(adjoint, (("space", 2),), 128)
        summed = face_sum(padded, face_jacobians, neighbours, jnp.zeros_like(adjoint))
        plane_rows = lax.all_gather(adjoint[:, :, :128], "space", axis=2, tiled=True)
        source = lax.dynamic_slice_in_dim(plane_rows, plane_source[0] * 128, 128, 2)
        plane_term = jnp.sum(plane_jacobians.astype(jnp.float32) * source[:, :, None, :], axis=1)
        summed = summed.at[:, :, :128].add(plane_term)
        gathered = lax.all_gather(adjoint, "inst", axis=0, tiled=True)
        spectral = jnp.einsum("mn,mbi->nbi", own_cols, gathered, precision=lax.Precision.HIGHEST)
        adjoint = apply_inverse(diagonal_inverse, objective_grad - summed - frequency * spectral)
    return adjoint


def solution(mesh):
    placed = (
        P("inst", None, "space"),
        P("inst", None, None, None, "space"),
        P("inst", None, None, "space"),
        P("inst", None, None, "space"),
        P(None, "space"),
        P("space"),
    )
    return jax.shard_map(
        body, mesh=mesh, in_specs=placed, out_specs=P("inst", None, "space"), check_vma=False
    )
```

profile of v0, /device:TPU:1, one launch (start us, length us, event | category | flops | bytes accessed | tf_op | source)
XLA Modules:
  0.0 337.2 jit_solution(3477753020776749565)
XLA Ops:
  0.0 1.3 multiply_reduce_fusion.4
  1.3 8.8 %collective-permute-start.1 = (f32[2,5,128]{2,0,1:T(2,128)S(1)}, f32[2,5,128]{2,0,1:T(2,128)S(1)}, u32[]{:S(2)}, u32[]{:S(2)}) collective-permute-start(f32[2,5,128]{2,0,1:T(2,128)S(1)} %get-tuple-element.316), channel_id=1, source_target_pairs={{1,0},{2,1},{3,2},{4,3},{5,4},{6,5},{7,6},{8,7},{9,8},{10,9},{11,1... | collective-permute-start | bytes 15368 | tf_op jit(solution)/shard_map/ppermute | solution.py:22
  10.1 1.9 collective-permute-start
  12.0 78.8 %all_gather.12 = f32[2,5,8192]{2,0,1:T(2,128)S(1)} all-gather(f32[2,5,128]{2,0,1:T(2,128)S(1)} %get-tuple-element.316), channel_id=1, replica_groups=mesh['inst'=8,'space'=64] {'space'}, dimensions={2}, use_global_device_ids=true | all-gather | bytes 332800 | tf_op jit(solution)/shard_map/all_gather | solution.py:74
  91.5 44.2 %all_gather.13 = f32[16,5,2048]{2,1,0:T(8,128)S(1)} all-gather(f32[2,5,2048]{2,1,0:T(8,128)S(1)} %copy.24), channel_id=1, replica_groups=mesh['inst'=8,'space'=64] {'inst'}, dimensions={0}, use_global_device_ids=true | all-gather | bytes 737280 | tf_op jit(solution)/shard_map/all_gather | solution.py:78
  135.9 36.2 %while.30 = (s32[]{:T(128)}, f32[2,5,2048]{2,0,1:T(2,128)S(1)}, f32[2,5,2304]{2,0,1:T(2,128)S(1)}, s32[6,2048]{1,0:T(8,128)}, bf16[2,6,5,5,2048]{4,0,3,2,1:T(2,1...) while((s32[]{:T(128)}, f32[2,5,2048]{2,0,1:T(2,128)S(1)}, ...), condition=%wide.region_2.3_spmd.clone, body=%wide.region_1.2_spmd.clone.sunk | while | flops 35799048 | bytes 283840 | solution.py:59
  135.9 0.7 dynamic-slice_subtract_fusion.4
  137.1 1.0 multiply_reduce_fusion.7
  139.4 1.0 multiply_reduce_fusion.7
  141.7 1.0 multiply_reduce_fusion.7
  142.7 0.7 dynamic-slice_subtract_fusion.4
  143.9 1.0 multiply_reduce_fusion.7
  146.2 1.0 multiply_reduce_fusion.7
  148.5 1.0 multiply_reduce_fusion.7
  150.7 1.0 multiply_reduce_fusion.7
  153.0 1.0 multiply_reduce_fusion.7
  155.2 1.0 multiply_reduce_fusion.7
  157.5 1.0 multiply_reduce_fusion.7
  159.8 1.0 multiply_reduce_fusion.7
  162.0 1.0 multiply_reduce_fusion.7
  164.3 1.0 multiply_reduce_fusion.7
  166.6 1.0 multiply_reduce_fusion.7
  168.8 1.0 multiply_reduce_fusion.7
  171.1 1.0 multiply_reduce_fusion.7
  172.1 0.8 fusion.19
  173.3 5.4 %collective-permute-start.3 = (f32[2,5,128]{2,0,1:T(2,128)S(1)}, f32[2,5,128]{2,0,1:T(2,128)S(1)}, u32[]{:S(2)}, u32[]{:S(2)}) collective-permute-start(f32[2,5,128]{2,0,1:T(2,128)S(1)} %get-tuple-element.314), channel_id=1, source_target_pairs={{1,0},{2,1},{3,2},{4,3},{5,4},{6,5},{7,6},{8,7},{9,8},{10,9},{11,1... | collective-permute-start | bytes 15368 | tf_op jit(solution)/shard_map/ppermute | solution.py:22
  178.8 75.8 %all_gather.14 = f32[2,5,8192]{2,0,1:T(2,128)S(1)} all-gather(f32[2,5,128]{2,0,1:T(2,128)S(1)} %get-tuple-element.314), channel_id=1, replica_groups=mesh['inst'=8,'space'=64] {'space'}, dimensions={2}, use_global_device_ids=true | all-gather | bytes 332800 | tf_op jit(solution)/shard_map/all_gather | solution.py:74
  254.6 2.3 collective-permute-start.2
  256.9 42.3 %all_gather.15 = f32[16,5,2048]{2,1,0:T(8,128)S(1)} all-gather(f32[2,5,2048]{2,1,0:T(8,128)S(1)} %copy.29), channel_id=1, replica_groups=mesh['inst'=8,'space'=64] {'inst'}, dimensions={0}, use_global_device_ids=true | all-gather | bytes 737280 | tf_op jit(solution)/shard_map/all_gather | solution.py:78
  299.3 36.2 %while.31 = (s32[]{:T(128)}, f32[2,5,2048]{2,0,1:T(2,128)S(1)}, f32[2,5,2304]{2,0,1:T(2,128)S(1)}, s32[6,2048]{1,0:T(8,128)}, bf16[2,6,5,5,2048]{4,0,3,2,1:T(2,1...) while((s32[]{:T(128)}, f32[2,5,2048]{2,0,1:T(2,128)S(1)}, ...), condition=%wide.region_6.7_spmd.clone, body=%wide.region_5.6_spmd.clone.sunk | while | flops 35799048 | bytes 283840 | solution.py:59
  300.5 1.0 multiply_reduce_fusion.8
  302.8 1.0 multiply_reduce_fusion.8
  305.1 1.0 multiply_reduce_fusion.8
  307.3 1.0 multiply_reduce_fusion.8
  309.6 1.0 multiply_reduce_fusion.8
  311.9 1.0 multiply_reduce_fusion.8
  314.1 1.0 multiply_reduce_fusion.8
  316.4 1.0 multiply_reduce_fusion.8
  318.6 1.0 multiply_reduce_fusion.8
  320.9 1.0 multiply_reduce_fusion.8
  323.2 1.0 multiply_reduce_fusion.8
  325.4 1.0 multiply_reduce_fusion.8
  327.7 1.0 multiply_reduce_fusion.8
  330.0 1.0 multiply_reduce_fusion.8
  332.2 1.0 multiply_reduce_fusion.8
  334.5 1.0 multiply_reduce_fusion.8
  335.5 0.8 fusion.18
  336.4 0.8 multiply_reduce_fusion.2
  (216 shorter events, 38.7 us)
Async XLA Ops:
  0.0 135.7 %copy-start.2 = (bf16[2,5,5,128]{3,0,2,1:T(2,128)(2,1)S(1)}, bf16[2,5,5,128]{3,0,2,1:T(2,128)(2,1)}, u32[]{:S(2)}) copy-start(bf16[2,5,5,128]{3,0,2,1:T(2,128)(2,1)} %param.16) | copy-start | bytes 38404
  1.3 134.5 %collective-permute-start.1 = (f32[2,5,128]{2,0,1:T(2,128)S(1)}, f32[2,5,128]{2,0,1:T(2,128)S(1)}, u32[]{:S(2)}, u32[]{:S(2)}) collective-permute-start(f32[2,5,128]{2,0,1:T(2,128)S(1)} %get-tuple-element.316), channel_id=1, source_target_pairs={{1,0},{2,1},{3,2},{4,3},{5,4},{6,5},{7,6},{8,7},{9,8},{10,9},{11,1... | collective-permute-start | bytes 15368 | tf_op jit(solution)/shard_map/ppermute | solution.py:22
  10.1 125.7 %collective-permute-start = (f32[2,5,128]{2,0,1:T(2,128)S(1)}, f32[2,5,128]{2,0,1:T(2,128)S(1)}, u32[]{:S(2)}, u32[]{:S(2)}) collective-permute-start(f32[2,5,128]{2,0,1:T(2,128)S(1)} %get-tuple-element.315), channel_id=1, source_target_pairs={{0,1},{1,2},{2,3},{3,4},{4,5},{5,6},{6,7},{7,8},{8,9},{9,10},{10,1... | collective-permute-start | bytes 15368 | tf_op jit(solution)/shard_map/ppermute | solution.py:21
  135.9 36.3 %copy-start.1 = (f32[2,5,2048]{2,0,1:T(2,128)S(1)}, f32[2,5,2048]{2,0,1:T(2,128)}, u32[]{:S(2)}) copy-start(f32[2,5,2048]{2,0,1:T(2,128)} %param.14) | copy-start | bytes 245764
  172.1 1.0 copy-start
  173.3 125.9 %collective-permute-start.3 = (f32[2,5,128]{2,0,1:T(2,128)S(1)}, f32[2,5,128]{2,0,1:T(2,128)S(1)}, u32[]{:S(2)}, u32[]{:S(2)}) collective-permute-start(f32[2,5,128]{2,0,1:T(2,128)S(1)} %get-tuple-element.314), channel_id=1, source_target_pairs={{1,0},{2,1},{3,2},{4,3},{5,4},{6,5},{7,6},{8,7},{9,8},{10,9},{11,1... | collective-permute-start | bytes 15368 | tf_op jit(solution)/shard_map/ppermute | solution.py:22
  254.6 44.6 %collective-permute-start.2 = (f32[2,5,128]{2,0,1:T(2,128)S(1)}, f32[2,5,128]{2,0,1:T(2,128)S(1)}, u32[]{:S(2)}, u32[]{:S(2)}) collective-permute-start(f32[2,5,128]{2,0,1:T(2,128)S(1)} %get-tuple-element.313), channel_id=1, source_target_pairs={{0,1},{1,2},{2,3},{3,4},{4,5},{5,6},{6,7},{7,8},{8,9},{9,10},{10,1... | collective-permute-start | bytes 15368 | tf_op jit(solution)/shard_map/ppermute | solution.py:21
where the time goes:
time: 342 us; the launch traced here: 337 us
  blocking collectives  241 us (70%)
  other arithmetic  56.5 us (17%)
  starting transfers between devices  18.4 us (5%)
  matrix products  17.3 us (5%)
    all_gather x2, blocking collectives, body(): lax.all_gather(adjoint[:, :, :128], 'space', axis=2, tiled=True)  155 us
    all_gather x2, blocking collectives, body(): gathered = lax.all_gather(adjoint, 'inst', axis=0, tiled=True)  86.5 us
    while x32, other arithmetic  31.8 us
    sub x32, other arithmetic, one_block(): local_idx = lax.dynamic_slice_in_dim(neighbours, start, 128, 1) - start  22.2 us
    dot_general x32, matrix products, one_block(): jnp.einsum('rw,kwc->rkc', window, onehot, precision=lax.Precision.HIGHEST)  15.7 us
    ppermute x2, starting transfers between devices, padded_2(): after = lax.ppermute(first, axis, down)  14.2 us
  transfers between devices with their start and end apart: 4, of which 0 were waited for; matrix products, arithmetic and copies ran while one was open for 0% of the time, Pallas kernels for 0%

commit v1 on v0

v1 whole, which is shorter than its diff:
```python
import functools
import math

import jax
import jax.numpy as jnp
from jax import lax
from jax.experimental import pallas as pl
from jax.experimental.pallas import tpu as pltpu
from jax.sharding import PartitionSpec as P

MESH = pl.DeviceIdType.MESH
F32 = jnp.float32

ITERS = 2
NT = 16
COMP = 5
FACES = 6
FREQUENCY = 0.05

ROWS = 32
CHUNKS = 4
TOP = 8


def spectral(diff):
    diff = diff % NT
    if diff == 0:
        return 0.0
    return FREQUENCY * 0.5 * (-1.0) ** diff / math.tan(math.pi * diff / NT)


def pick(position, values):
    out = jnp.float32(values[-1])
    for i in range(len(values) - 1):
        out = jnp.where(position == i, jnp.float32(values[i]), out)
    return out


def kernel(
    grad_hbm, face_hbm, plane_hbm, inv_hbm, nb_hbm, src_ref, out_hbm,
    grad, face, plane, inv, nb, lane, side, win, summed, own, xbuf, zsend, zrecv,
    edge, halo, prow, psend, pcol, tab,
    load_sem, xs_sem, xr_sem, zs_sem, zr_sem, hs_sem, hr_sem, as_sem, ar_sem, bs_sem, br_sem, ts_sem, tr_sem,
):
    q, d = lax.axis_index("inst"), lax.axis_index("space")
    half, x = q // 4, lax.rem(q, 4)
    zlo, y, core = d // 16, lax.rem(d, 16) // 2, lax.rem(d, 2)
    col = zlo * 2 + core

    loads = [
        pltpu.make_async_copy(src, dst, load_sem.at[i])
        for i, (src, dst) in enumerate(
            [(grad_hbm, grad), (inv_hbm, inv), (nb_hbm, nb), (plane_hbm, plane), (face_hbm, face)]
        )
    ]
    for load in loads:
        load.start()

    def x_peer(i):
        return (half * 4 + lax.rem(x + i, 4), d)

    z_peer = (lax.rem(q + 4, 8), d)
    before, after = (q, lax.rem(d + 63, 64)), (q, lax.rem(d + 1, 64))

    def y_peer(i):
        return (q, zlo * 16 + lax.rem(y + i, 8) * 2 + core)

    def col_of(i):
        return lax.rem(col + i, 8)

    def col_peer(i):
        other = col_of(i)
        return (q, other // 2 * 16 + y * 2 + lax.rem(other, 2))

    partners = [x_peer(i) for i in (1, 2, 3)] + [z_peer, before, after]
    partners += [y_peer(i) for i in range(1, 8)] + [col_peer(i) for i in range(1, 8)]
    barrier = pltpu.get_barrier_semaphore()
    for p in partners:
        pl.semaphore_signal(barrier, inc=1, device_id=p, device_id_type=MESH)

    def x_copy(s, i, j):
        rows = pl.ds(8 * j, 8)
        return pltpu.make_async_remote_copy(
            src_ref=xbuf.at[s, x, :, rows], dst_ref=xbuf.at[s, x, :, rows],
            send_sem=xs_sem.at[s, i, j], recv_sem=xr_sem.at[s, x, j],
            device_id=x_peer(i), device_id_type=MESH,
        )

    def x_arrival(s, i, j):
        rows, slot = pl.ds(8 * j, 8), lax.rem(x + i, 4)
        return pltpu.make_async_remote_copy(
            src_ref=xbuf.at[s, slot, :, rows], dst_ref=xbuf.at[s, slot, :, rows],
            send_sem=xs_sem.at[s, i, j], recv_sem=xr_sem.at[s, slot, j],
            device_id=x_peer(i), device_id_type=MESH,
        )

    def z_copy(s, j):
        rows = pl.ds(8 * j, 8)
        return pltpu.make_async_remote_copy(
            src_ref=zsend.at[s, :, rows], dst_ref=zrecv.at[s, :, rows],
            send_sem=zs_sem.at[s, j], recv_sem=zr_sem.at[s, j],
            device_id=z_peer, device_id_type=MESH,
        )

    def halo_copy(s, e):
        return pltpu.make_async_remote_copy(
            src_ref=edge.at[s, e], dst_ref=halo.at[s, 1 - e],
            send_sem=hs_sem.at[s, e], recv_sem=hr_sem.at[s, 1 - e],
            device_id=after if e else before, device_id_type=MESH,
        )

    def row_copy(s, i, slot):
        return pltpu.make_async_remote_copy(
            src_ref=edge.at[s, 0], dst_ref=prow.at[s, slot],
            send_sem=as_sem.at[s, i], recv_sem=ar_sem.at[s, slot],
            device_id=y_peer(i), device_id_type=MESH,
        )

    def col_copy(s, i, slot):
        return pltpu.make_async_remote_copy(
            src_ref=psend.at[s, i], dst_ref=pcol.at[s, slot],
            send_sem=bs_sem.at[s, i], recv_sem=br_sem.at[s, slot],
            device_id=col_peer(i), device_id_type=MESH,
        )

    def tab_copy(i, slot):
        return pltpu.make_async_remote_copy(
            src_ref=tab.at[8], dst_ref=tab.at[slot],
            send_sem=ts_sem.at[i], recv_sem=tr_sem.at[slot],
            device_id=col_peer(i), device_id_type=MESH,
        )

    odd = lax.rem(lax.broadcasted_iota(jnp.int32, (8, 128), 0), 2) == 1
    coef = []
    for base in (0, 8):
        straight, crossed = [], []
        for other in range(4):
            steps = [2 * (other - me) + base for me in range(4)]
            straight.append(pick(x, [spectral(e) for e in steps]))
            crossed.append(
                jnp.where(odd, pick(x, [spectral(e + 1) for e in steps]), pick(x, [spectral(e - 1) for e in steps]))
            )
        coef.append((straight, crossed))

    def swap(v):
        return jnp.where(odd, pltpu.roll(v, 1, 0), pltpu.roll(v, 7, 0))

    def publish(s, j, value):
        for c in range(COMP):
            win[s, c, pl.ds(TOP + 8 * j, 8), :] = value[c]
            xbuf[s, x, c, pl.ds(8 * j, 8), :] = value[c]
        if s == 0 and j == 0:
            pl.semaphore_wait(barrier, len(partners))
            for i in range(1, 8):
                tab_copy(i, col).start()
        if j == 0:
            for c in range(COMP):
                edge[s, 0, 2 * c : 2 * c + 2, :] = value[c][0:2]
            prow[s, y] = edge[s, 0]
            for i in range(1, 8):
                row_copy(s, i, y).start()
            halo_copy(s, 0).start()
        if j == CHUNKS - 1:
            for c in range(COMP):
                edge[s, 1, 2 * c : 2 * c + 2, :] = value[c][6:8]
            halo_copy(s, 1).start()
        for i in (2, 1, 3):
            x_copy(s, i, j).start()

    def apply_inverse(j, values):
        rows = pl.ds(8 * j, 8)
        out = []
        for c in range(COMP):
            total = inv[0, c, rows, :] * values[0]
            for b in range(1, COMP):
                total = total + inv[b, c, rows, :] * values[b]
            out.append(total)
        return out

    def faces(s, j):
        rows = pl.ds(8 * j, 8)
        tall = pl.ds(16 * (j // 2), 16)
        lower = 8 * (j % 2)

        def one_face(k, total):
            at, where = lane[k, rows, :], side[k, rows, :]
            total = list(total)
            for a in range(COMP):
                got = [
                    jnp.take_along_axis(
                        win[s, a, pl.ds(TOP + 8 * j + 2 * o, 8), :], at, axis=1, mode="promise_in_bounds"
                    )
                    for o in (-1, 0, 1)
                ]
                beside = jnp.where(where == 0, got[0], jnp.where(where == 1, got[1], got[2]))
                for b in range(COMP):
                    jac = face[k, a, b, tall, :].astype(F32)[lower : lower + 8]
                    total[b] = total[b] + jac * beside
            return tuple(total)

        total = lax.fori_loop(0, FACES, one_face, tuple(jnp.zeros((8, 128), F32) for _ in range(COMP)))
        for b in range(COMP):
            summed[b, rows, :] = total[b]

    def instances(s, j):
        rows = pl.ds(8 * j, 8)
        for i in (1, 3, 2):
            x_arrival(s, i, j).wait_recv()
        for a in range(COMP):
            values = [xbuf[s, other, a, rows, :] for other in range(4)]
            sums = []
            for straight, crossed in coef:
                plain = straight[0] * values[0]
                turned = crossed[0] * values[0]
                for other in range(1, 4):
                    plain = plain + straight[other] * values[other]
                    turned = turned + crossed[other] * values[other]
                sums.append(plain + swap(turned))
            own[a, rows, :] = sums[0]
            zsend[s, a, rows, :] = sums[1]
        z_copy(s, j).start()

    tab[8] = jnp.full((1, 128), src_ref[0], jnp.int32)
    tab[col] = jnp.full((1, 128), src_ref[0], jnp.int32)
    loads[0].wait()
    loads[1].wait()
    for j in range(CHUNKS):
        publish(0, j, apply_inverse(j, [grad[b, pl.ds(8 * j, 8), :] for b in range(COMP)]))

    loads[2].wait()
    for k in range(FACES):
        for block in range(ROWS // 2):
            index = nb[k : k + 1, 128 * block : 128 * block + 128] - 128 * block
            lane[k, 2 * block : 2 * block + 2, :] = jnp.broadcast_to(index & 127, (2, 128))
            side[k, 2 * block : 2 * block + 2, :] = jnp.broadcast_to(index >> 7, (2, 128))
    loads[3].wait()
    loads[4].wait()

    out_copies = []
    for s in range(ITERS):
        for j in (1, 2):
            faces(s, j)
        for j in range(CHUNKS):
            instances(s, j)

        for i in range(1, 8):
            slot = lax.rem(y + i, 8)
            row_copy(s, i, slot).wait_recv()
        if s == 0:
            for i in range(1, 8):
                tab_copy(i, col_of(i)).wait_recv()
        blocks = [prow[s, r] for r in range(8)]
        for i in range(8):
            want = jnp.broadcast_to(lax.rem(tab[col_of(i)], 16) // 2, (16, 128))
            chosen = blocks[7]
            for r in range(7):
                chosen = jnp.where(want == r, blocks[r], chosen)
            if i == 0:
                pcol[s, col] = chosen
            else:
                psend[s, i] = chosen
                col_copy(s, i, col).start()

        for e in (0, 1):
            halo_copy(s, e).wait_recv()
        for c in range(COMP):
            win[s, c, TOP - 2 : TOP, :] = halo[s, 0, 2 * c : 2 * c + 2, :]
            win[s, c, TOP + ROWS : TOP + ROWS + 2, :] = halo[s, 1, 2 * c : 2 * c + 2, :]
        for j in (0, 3):
            faces(s, j)

        for i in range(1, 8):
            col_copy(s, i, col_of(i)).wait_recv()
        mine = tab[8]
        want = jnp.broadcast_to(mine // 16 * 2 + lax.rem(mine, 2), (16, 128))
        source = pcol[s, 7]
        for r in range(7):
            source = jnp.where(want == r, pcol[s, r], source)
        for b in range(COMP):
            term = summed[b, 0:2, :]
            for a in range(COMP):
                term = term + plane[a, b].astype(F32) * source[2 * a : 2 * a + 2]
            summed[b, 0:2, :] = term

        for j in range(CHUNKS):
            rows = pl.ds(8 * j, 8)
            z_copy(s, j).wait_recv()
            right = [
                grad[b, rows, :] - summed[b, rows, :] - (own[b, rows, :] + zrecv[s, b, rows, :]) for b in range(COMP)
            ]
            value = apply_inverse(j, right)
            if s + 1 < ITERS:
                publish(s + 1, j, value)
            else:
                for c in range(COMP):
                    win[s + 1, c, rows, :] = value[c]
                copy = pltpu.make_async_copy(win.at[s + 1, :, rows], out_hbm.at[:, rows], load_sem.at[j])
                copy.start()
                out_copies.append(copy)

    for i in range(1, 8):
        tab_copy(i, col).wait_send()
    for s in range(ITERS):
        for j in range(CHUNKS):
            for i in (1, 2, 3):
                x_copy(s, i, j).wait_send()
            z_copy(s, j).wait_send()
        for e in (0, 1):
            halo_copy(s, e).wait_send()
        for i in range(1, 8):
            row_copy(s, i, y).wait_send()
            col_copy(s, i, col).wait_send()
    for copy in out_copies:
        copy.wait()


def body(objective_grad, face_jacobians, plane_jacobians, diagonal_inverse, neighbours, plane_source):
    blocks = ROWS // 2
    grad = objective_grad.reshape(2, COMP, blocks, 128).transpose(1, 2, 0, 3).reshape(COMP, ROWS, 128)
    face = face_jacobians.reshape(2, FACES, COMP, COMP, blocks, 128)
    face = face.transpose(1, 2, 3, 4, 0, 5).reshape(FACES, COMP, COMP, ROWS, 128)
    inv = diagonal_inverse.reshape(2, COMP, COMP, blocks, 128)
    inv = inv.transpose(1, 2, 3, 0, 4).reshape(COMP, COMP, ROWS, 128)
    plane = plane_jacobians.transpose(1, 2, 0, 3)
    anywhere = pl.BlockSpec(memory_space=pl.ANY)
    dma = pltpu.SemaphoreType.DMA
    out = pl.pallas_call(
        kernel,
        out_shape=jax.ShapeDtypeStruct((COMP, ROWS, 128), F32),
        in_specs=[anywhere] * 5 + [pl.BlockSpec(memory_space=pltpu.SMEM)],
        out_specs=anywhere,
        scratch_shapes=[
            pltpu.VMEM((COMP, ROWS, 128), F32),
            pltpu.VMEM((FACES, COMP, COMP, ROWS, 128), jnp.bfloat16),
            pltpu.VMEM((COMP, COMP, 2, 128), jnp.bfloat16),
            pltpu.VMEM((COMP, COMP, ROWS, 128), F32),
            pltpu.VMEM((FACES, 2048), jnp.int32),
            pltpu.VMEM((FACES, ROWS, 128), jnp.int32),
            pltpu.VMEM((FACES, ROWS, 128), jnp.int32),
            pltpu.VMEM((ITERS + 1, COMP, ROWS + 2 * TOP, 128), F32),
            pltpu.VMEM((COMP, ROWS, 128), F32),
            pltpu.VMEM((COMP, ROWS, 128), F32),
            pltpu.VMEM((ITERS, 4, COMP, ROWS, 128), F32),
            pltpu.VMEM((ITERS, COMP, ROWS, 128), F32),
            pltpu.VMEM((ITERS, COMP, ROWS, 128), F32),
            pltpu.VMEM((ITERS, 2, 16, 128), F32),
            pltpu.VMEM((ITERS, 2, 16, 128), F32),
            pltpu.VMEM((ITERS, 8, 16, 128), F32),
            pltpu.VMEM((ITERS, 8, 16, 128), F32),
            pltpu.VMEM((ITERS, 8, 16, 128), F32),
            pltpu.VMEM((9, 1, 128), jnp.int32),
            dma((5,)),
            dma((ITERS, 4, CHUNKS)), dma((ITERS, 4, CHUNKS)),
            dma((ITERS, CHUNKS)), dma((ITERS, CHUNKS)),
            dma((ITERS, 2)), dma((ITERS, 2)),
            dma((ITERS, 8)), dma((ITERS, 8)),
            dma((ITERS, 8)), dma((ITERS, 8)),
            dma((8,)), dma((8,)),
        ],
        compiler_params=pltpu.CompilerParams(
            collective_id=0, has_side_effects=True, vmem_limit_bytes=48 * 1024 * 1024
        ),
    )(grad, face, plane, inv, neighbours, plane_source)
    return out.reshape(COMP, blocks, 2, 128).transpose(2, 0, 1, 3).reshape(2, COMP, 2048)


def solution(mesh):
    placed = (
        P("inst", None, "space"),
        P("inst", None, None, None, "space"),
        P("inst", None, None, "space"),
        P("inst", None, None, "space"),
        P(None, "space"),
        P("space"),
    )
    return jax.shard_map(
        body, mesh=mesh, in_specs=placed, out_specs=P("inst", None, "space"), check_vma=False
    )
```

time: 342 us -> 45.4 us (0.13); the launches traced: 337 us -> 45.1 us
  blocking collectives: 241 us -> 0 us
  other arithmetic: 56.5 us -> 0 us
  Pallas kernels: 0 us -> 39 us
  starting transfers between devices: 18.4 us -> 0 us
  matrix products: 17.3 us -> 0 us
  local copies, waits for them, and re-layouts: 1.81 us -> 5.35 us
    all_gather x4 -> x0, blocking collectives: 241 us -> none  [the longest x2 155 us: body(): lax.all_gather(adjoint[:, :, :128], 'space', axis=2, tiled=True)]
    pallas_call x0 -> x1, Pallas kernels: none -> 39 us  [body(): pl.pallas_call(kernel, out_shape=jax.ShapeDtypeStruct((COMP, ROWS, 128),...]
    while x32 -> x0, other arithmetic: 31.8 us -> none
    sub x32 -> x0, other arithmetic: 22.2 us -> none  [one_block(): local_idx = lax.dynamic_slice_in_dim(neighbours, start, 128, 1) - start]
    ppermute x4 -> x0, starting transfers between devices: 18.4 us -> none  [the longest x2 14.2 us: padded_2(): after = lax.ppermute(first, axis, down)]
    dot_general x34 -> x0, matrix products: 17.3 us -> none  [the longest x32 15.7 us: one_block(): jnp.einsum('rw,kwc->rkc', window, onehot, precision=lax.Precision.HIGHEST)]
    unnamed x6 -> x11, local copies, waits for them, and re-layouts: 0.15 us -> 5.35 us
  transfers between devices with their start and end apart: 4 -> 0, of which waited for: 0 -> 0; matrix products, arithmetic and copies ran while one was open for 0% -> 0% of each run, Pallas kernels for 0% -> 0%
where the time goes in v1:
time: 45.4 us; the launch traced here: 45.1 us
  Pallas kernels  39 us (86%)
  local copies, waits for them, and re-layouts  5.35 us (12%)
  between operations  0.67 us (1%)
    pallas_call x1, Pallas kernels, body(): pl.pallas_call(kernel, out_shape=jax.ShapeDtypeStruct((COMP, ROWS, 128),...  39 us
    unnamed x11, local copies, waits for them, and re-layouts  5.35 us

profile of v1, /device:TPU:1, one launch (start us, length us, event | category | flops | bytes accessed | tf_op | source)
XLA Modules:
  0.0 45.1 jit_solution(2892889343317194746)
XLA Ops:
  0.7 0.0 copy-start
  0.7 1.3 %copy-done = bf16[2,6,5,5,2048]{4,0,3,2,1:T(2,128)(2,1)S(1)} copy-done((bf16[2,6,5,5,2048]{4,0,3,2,1:T(2,128)(2,1)S(1)}, bf16[2,6,5,5,2048]{4,0,3,2,1:T(2,128)(2,1)}, u32[]{:S(2)}) %copy-start) | copy-done | bytes 1228824
  1.9 0.0 copy-start.1
  1.9 1.0 %copy-done.1 = f32[2,5,5,2048]{3,0,2,1:T(2,128)S(1)} copy-done((f32[2,5,5,2048]{3,0,2,1:T(2,128)S(1)}, f32[2,5,5,2048]{3,0,2,1:T(2,128)}, u32[]{:S(2)}) %copy-start.1) | copy-done | bytes 409624
  2.9 0.0 copy-start.2
  2.9 0.9 %copy-done.2 = f32[2,5,2048]{2,0,1:T(2,128)S(1)} copy-done((f32[2,5,2048]{2,0,1:T(2,128)S(1)}, f32[2,5,2048]{2,0,1:T(2,128)}, u32[]{:S(2)}) %copy-start.2) | copy-done | bytes 81944
  3.8 0.0 copy-start.3
  3.8 0.8 %copy-done.3 = s32[6,2048]{1,0:T(8,128)S(1)} copy-done((s32[6,2048]{1,0:T(8,128)S(1)}, s32[6,2048]{1,0:T(8,128)}, u32[]{:S(2)}) %copy-start.3) | copy-done | bytes 49176
  4.7 0.0 copy-start.4
  4.7 0.7 %copy-done.4 = bf16[2,5,5,128]{3,0,2,1:T(2,128)(2,1)S(1)} copy-done((bf16[2,5,5,128]{3,0,2,1:T(2,128)(2,1)S(1)}, bf16[2,5,5,128]{3,0,2,1:T(2,128)(2,1)}, u32[]{:S(2)}) %copy-start.4) | copy-done | bytes 12824
  5.4 39.0 %shard_map.64 = f32[5,32,128]{2,1,0:T(8,128)S(1)} custom-call(f32[5,32,128]{2,1,0:T(8,128)S(1)} %bitcast.24, bf16[6,5,5,32,128]{4,3,2,1,0:T(8,128)(2,1)S(1)} %bitcast.21, bf16[5,5,2,128]{3,2,1,0:T(2,128)(2,1)S(1)} %bitcast.25, f32[5,5,32,128]{3,2,1,0:T(8,128)S(1)} %bitcast.22, s32[6,2048]{1,0:T(8,128)S(1)} %copy-done.3, s32[1]{0:T(128)S(6)} %copy.12.src_ref), custom_call_target="tpu_custom_call" | custom-call | tf_op jit(solution)/shard_map/pallas_call | solution.py:327
  44.4 0.6 %copy.13 = f32[2,5,2048]{2,0,1:T(2,128)} copy(f32[2,5,2048]{2,0,1:T(2,128)S(1)} %bitcast.23) | data formatting | bytes 163840
Async XLA Ops:
  0.7 1.3 %copy-start = (bf16[2,6,5,5,2048]{4,0,3,2,1:T(2,128)(2,1)S(1)}, bf16[2,6,5,5,2048]{4,0,3,2,1:T(2,128)(2,1)}, u32[]{:S(2)}) copy-start(bf16[2,6,5,5,2048]{4,0,3,2,1:T(2,128)(2,1)} %param.7) | copy-start | bytes 3686404
  1.9 1.0 %copy-start.1 = (f32[2,5,5,2048]{3,0,2,1:T(2,128)S(1)}, f32[2,5,5,2048]{3,0,2,1:T(2,128)}, u32[]{:S(2)}) copy-start(f32[2,5,5,2048]{3,0,2,1:T(2,128)} %param.9) | copy-start | bytes 1228804
  2.9 0.9 %copy-start.2 = (f32[2,5,2048]{2,0,1:T(2,128)S(1)}, f32[2,5,2048]{2,0,1:T(2,128)}, u32[]{:S(2)}) copy-start(f32[2,5,2048]{2,0,1:T(2,128)} %param.6) | copy-start | bytes 245764
  3.8 0.8 %copy-start.3 = (s32[6,2048]{1,0:T(8,128)S(1)}, s32[6,2048]{1,0:T(8,128)}, u32[]{:S(2)}) copy-start(s32[6,2048]{1,0:T(8,128)} %nb_hbm.1) | copy-start | bytes 147460
  4.7 0.7 %copy-start.4 = (bf16[2,5,5,128]{3,0,2,1:T(2,128)(2,1)S(1)}, bf16[2,5,5,128]{3,0,2,1:T(2,128)(2,1)}, u32[]{:S(2)}) copy-start(bf16[2,5,5,128]{3,0,2,1:T(2,128)(2,1)} %param.8) | copy-start | bytes 38404

commit v2 on v1

--- a/solution.py
+++ b/solution.py
@@ -198,7 +198,7 @@
                     total[b] = total[b] + jac * beside
             return tuple(total)
 
-        total = lax.fori_loop(0, FACES, one_face, tuple(jnp.zeros((8, 128), F32) for _ in range(COMP)))
+        total = lax.fori_loop(0, FACES, one_face, tuple(jnp.zeros((8, 128), F32) for _ in range(COMP)), unroll=True)
         for b in range(COMP):
             summed[b, rows, :] = total[b]
 
@@ -358,7 +358,7 @@
             dma((8,)), dma((8,)),
         ],
         compiler_params=pltpu.CompilerParams(
-            collective_id=0, has_side_effects=True, vmem_limit_bytes=48 * 1024 * 1024
+            collective_id=0, has_side_effects=True, vmem_limit_bytes=60 * 1024 * 1024
         ),
     )(grad, face, plane, inv, neighbours, plane_source)
     return out.reshape(COMP, blocks, 2, 128).transpose(2, 0, 1, 3).reshape(2, COMP, 2048)

time: 45.4 us -> 41.2 us (0.907)
  local copies, waits for them, and re-layouts: 5.35 us -> 1.53 us
    unnamed x11 -> x1, local copies, waits for them, and re-layouts: 5.35 us -> 1.53 us
where the time goes in v2:
time: 41.2 us; the launch traced here: 41 us
  Pallas kernels  38.8 us (94%)
  local copies, waits for them, and re-layouts  1.53 us (4%)
  between operations  0.66 us (2%)
    pallas_call x1, Pallas kernels, body(): pl.pallas_call(kernel, out_shape=jax.ShapeDtypeStruct((COMP, ROWS, 128),...  38.8 us
    unnamed x1, local copies, waits for them, and re-layouts  1.53 us

profile of v2, /device:TPU:1, one launch (start us, length us, event | category | flops | bytes accessed | tf_op | source)
XLA Modules:
  0.0 41.0 jit_solution(17419470850252028037)
XLA Ops:
  0.7 38.8 %shard_map.64 = f32[5,32,128]{2,1,0:T(8,128)} custom-call(f32[5,32,128]{2,1,0:T(8,128)} %bitcast.24, bf16[6,5,5,32,128]{4,3,2,1,0:T(8,128)(2,1)} %bitcast.21, bf16[5,5,2,128]{3,2,1,0:T(2,128)(2,1)} %bitcast.25, f32[5,5,32,128]{3,2,1,0:T(8,128)} %bitcast.22, s32[6,2048]{1,0:T(8,128)} %nb_hbm.1, s32[1]{0:T(128)S(6)} %copy.12.src_ref), custom_call_target="tpu_custom_call" | custom-call | tf_op jit(solution)/shard_map/pallas_call | solution.py:327
  39.5 1.5 %copy.13 = f32[2,5,2048]{2,0,1:T(2,128)} copy(f32[2,5,2048]{2,0,1:T(2,128)} %bitcast.23) | data formatting | bytes 163840

commit v3 on v2

--- a/solution.py
+++ b/solution.py
@@ -37,10 +37,10 @@
 
 
 def kernel(
-    grad_hbm, face_hbm, plane_hbm, inv_hbm, nb_hbm, src_ref, out_hbm,
+    grad_hbm, face_hbm, plane_hbm, inv_hbm, nb_hbm, src_ref, out_ref,
     grad, face, plane, inv, nb, lane, side, win, summed, own, xbuf, zsend, zrecv,
-    edge, halo, prow, psend, pcol, tab,
-    load_sem, xs_sem, xr_sem, zs_sem, zr_sem, hs_sem, hr_sem, as_sem, ar_sem, bs_sem, br_sem, ts_sem, tr_sem,
+    edge, halo, prow, psend, pcol, ibuf, tab,
+    load_sem, xs_sem, xr_sem, zs_sem, zr_sem, hs_sem, hr_sem, as_sem, ar_sem, bs_sem, br_sem, is_sem, ir_sem, ts_sem, tr_sem, met_sem,
 ):
     q, d = lax.axis_index("inst"), lax.axis_index("space")
     half, x = q // 4, lax.rem(q, 4)
@@ -60,6 +60,7 @@
         return (half * 4 + lax.rem(x + i, 4), d)
 
     z_peer = (lax.rem(q + 4, 8), d)
+
     before, after = (q, lax.rem(d + 63, 64)), (q, lax.rem(d + 1, 64))
 
     def y_peer(i):
@@ -72,11 +73,28 @@
         other = col_of(i)
         return (q, other // 2 * 16 + y * 2 + lax.rem(other, 2))
 
-    partners = [x_peer(i) for i in (1, 2, 3)] + [z_peer, before, after]
+    partners = [x_peer(i) for i in (1, 2, 3)] + [before, after]
     partners += [y_peer(i) for i in range(1, 8)] + [col_peer(i) for i in range(1, 8)]
+    across = [((1 - half) * 4 + other, d) for other in range(4)]
     barrier = pltpu.get_barrier_semaphore()
     for p in partners:
         pl.semaphore_signal(barrier, inc=1, device_id=p, device_id_type=MESH)
+
+    @pl.when(half == 0)
+    def _():
+        for p in across:
+            pl.semaphore_signal(barrier, inc=1, device_id=p, device_id_type=MESH)
+
+    def enter():
+        @pl.when(half == 0)
+        def _():
+            pl.semaphore_wait(barrier, len(partners))
+
+        @pl.when(half == 1)
+        def _():
+            pl.semaphore_wait(barrier, len(partners) + len(across))
+            for p in across:
+                pl.semaphore_signal(met_sem, inc=1, device_id=p, device_id_type=MESH)
 
     def x_copy(s, i, j):
         rows = pl.ds(8 * j, 8)
@@ -142,33 +160,66 @@
             )
         coef.append((straight, crossed))
 
-    def swap(v):
-        return jnp.where(odd, pltpu.roll(v, 1, 0), pltpu.roll(v, 7, 0))
+    tall_odd = lax.rem(lax.broadcasted_iota(jnp.int32, (16, 128), 0), 2) == 1
+
+    def swap(v, mask):
+        return jnp.where(mask, pltpu.roll(v, 1, 0), pltpu.roll(v, v.shape[0] - 1, 0))
+
+    def cross_copy(s, other, slot):
+        return pltpu.make_async_remote_copy(
+            src_ref=edge.at[s, 0], dst_ref=ibuf.at[s, slot],
+            send_sem=is_sem.at[s, other], recv_sem=ir_sem.at[s, slot],
+            device_id=across[other], device_id_type=MESH,
+        )
+
+    def near_copy(s, i, slot):
+        return pltpu.make_async_remote_copy(
+            src_ref=edge.at[s, 0], dst_ref=ibuf.at[s, slot],
+            send_sem=is_sem.at[s, 4 + i], recv_sem=ir_sem.at[s, slot],
+            device_id=x_peer(i), device_id_type=MESH,
+        )
+
+    def send_across(s):
+        for other in range(4):
+            cross_copy(s, other, q).start()
+
+    def send_first(s, held):
+        if held:
+            pl.when(half == 1)(lambda: send_across(s))
+        else:
+            send_across(s)
+        for i in (2, 1, 3):
+            near_copy(s, i, q).start()
+
+    def publish_first(s, value):
+        for c in range(COMP):
+            win[s, c, TOP : TOP + 2, :] = value[c]
+            edge[s, 0, 2 * c : 2 * c + 2, :] = value[c]
+        if s == 0:
+            enter()
+        send_first(s, s == 0)
+        for i in (4, 3, 5, 2, 6, 1, 7):
+            row_copy(s, i, y).start()
+        halo_copy(s, 0).start()
+        block = edge[s, 0]
+        ibuf[s, q] = block
+        prow[s, y] = block
 
     def publish(s, j, value):
         for c in range(COMP):
-            win[s, c, pl.ds(TOP + 8 * j, 8), :] = value[c]
+            if j == 0:
+                win[s, c, TOP + 2 : TOP + 8, :] = value[c][2:]
+            else:
+                win[s, c, pl.ds(TOP + 8 * j, 8), :] = value[c]
             xbuf[s, x, c, pl.ds(8 * j, 8), :] = value[c]
-        if s == 0 and j == 0:
-            pl.semaphore_wait(barrier, len(partners))
-            for i in range(1, 8):
-                tab_copy(i, col).start()
-        if j == 0:
-            for c in range(COMP):
-                edge[s, 0, 2 * c : 2 * c + 2, :] = value[c][0:2]
-            prow[s, y] = edge[s, 0]
-            for i in range(1, 8):
-                row_copy(s, i, y).start()
-            halo_copy(s, 0).start()
+        for i in (2, 1, 3):
+            x_copy(s, i, j).start()
         if j == CHUNKS - 1:
             for c in range(COMP):
                 edge[s, 1, 2 * c : 2 * c + 2, :] = value[c][6:8]
             halo_copy(s, 1).start()
-        for i in (2, 1, 3):
-            x_copy(s, i, j).start()
-
-    def apply_inverse(j, values):
-        rows = pl.ds(8 * j, 8)
+
+    def apply_inverse(rows, values):
         out = []
         for c in range(COMP):
             total = inv[0, c, rows, :] * values[0]
@@ -202,7 +253,7 @@
         for b in range(COMP):
             summed[b, rows, :] = total[b]
 
-    def instances(s, j):
+    def instances(s, j, send=True):
         rows = pl.ds(8 * j, 8)
         for i in (1, 3, 2):
             x_arrival(s, i, j).wait_recv()
@@ -215,17 +266,23 @@
                 for other in range(1, 4):
                     plain = plain + straight[other] * values[other]
                     turned = turned + crossed[other] * values[other]
-                sums.append(plain + swap(turned))
+                sums.append(plain + swap(turned, odd))
             own[a, rows, :] = sums[0]
             zsend[s, a, rows, :] = sums[1]
-        z_copy(s, j).start()
+        if send:
+            z_copy(s, j).start()
 
     tab[8] = jnp.full((1, 128), src_ref[0], jnp.int32)
     tab[col] = jnp.full((1, 128), src_ref[0], jnp.int32)
     loads[0].wait()
     loads[1].wait()
     for j in range(CHUNKS):
-        publish(0, j, apply_inverse(j, [grad[b, pl.ds(8 * j, 8), :] for b in range(COMP)]))
+        value = apply_inverse(pl.ds(8 * j, 8), [grad[b, pl.ds(8 * j, 8), :] for b in range(COMP)])
+        if j == 0:
+            publish_first(0, [v[0:2] for v in value])
+            for i in range(1, 8):
+                tab_copy(i, col).start()
+        publish(0, j, value)
 
     loads[2].wait()
     for k in range(FACES):
@@ -236,22 +293,15 @@
     loads[3].wait()
     loads[4].wait()
 
-    out_copies = []
-    for s in range(ITERS):
-        for j in (1, 2):
-            faces(s, j)
-        for j in range(CHUNKS):
-            instances(s, j)
-
+    def select(s):
         for i in range(1, 8):
-            slot = lax.rem(y + i, 8)
-            row_copy(s, i, slot).wait_recv()
+            row_copy(s, i, lax.rem(y + i, 8)).wait_recv()
         if s == 0:
             for i in range(1, 8):
                 tab_copy(i, col_of(i)).wait_recv()
         blocks = [prow[s, r] for r in range(8)]
-        for i in range(8):
-            want = jnp.broadcast_to(lax.rem(tab[col_of(i)], 16) // 2, (16, 128))
+        for i in (4, 3, 5, 2, 6, 1, 7, 0):
+            want = jnp.broadcast_to((tab[col_of(i)] >> 1) & 7, (16, 128))
             chosen = blocks[7]
             for r in range(7):
                 chosen = jnp.where(want == r, blocks[r], chosen)
@@ -261,6 +311,7 @@
                 psend[s, i] = chosen
                 col_copy(s, i, col).start()
 
+    def halos(s):
         for e in (0, 1):
             halo_copy(s, e).wait_recv()
         for c in range(COMP):
@@ -269,34 +320,103 @@
         for j in (0, 3):
             faces(s, j)
 
+    def finish(s, j):
+        rows = pl.ds(8 * j, 8)
+        z_copy(s, j).wait_recv()
+        right = [
+            grad[b, rows, :] - summed[b, rows, :] - (own[b, rows, :] + zrecv[s, b, rows, :]) for b in range(COMP)
+        ]
+        value = apply_inverse(rows, right)
+        if s + 1 < ITERS:
+            publish(s + 1, j, value)
+        else:
+            for c in range(COMP):
+                if j == 0:
+                    out_ref[c, 2:8, :] = value[c][2:]
+                else:
+                    out_ref[c, rows, :] = value[c]
+
+    def finish_first(s):
         for i in range(1, 8):
             col_copy(s, i, col_of(i)).wait_recv()
         mine = tab[8]
-        want = jnp.broadcast_to(mine // 16 * 2 + lax.rem(mine, 2), (16, 128))
+        want = jnp.broadcast_to((mine >> 4) * 2 + (mine & 1), (16, 128))
         source = pcol[s, 7]
         for r in range(7):
             source = jnp.where(want == r, pcol[s, r], source)
+        terms = []
         for b in range(COMP):
-            term = summed[b, 0:2, :]
+            term = grad[b, 0:2, :] - summed[b, 0:2, :]
             for a in range(COMP):
-                term = term + plane[a, b].astype(F32) * source[2 * a : 2 * a + 2]
-            summed[b, 0:2, :] = term
-
-        for j in range(CHUNKS):
-            rows = pl.ds(8 * j, 8)
-            z_copy(s, j).wait_recv()
-            right = [
-                grad[b, rows, :] - summed[b, rows, :] - (own[b, rows, :] + zrecv[s, b, rows, :]) for b in range(COMP)
-            ]
-            value = apply_inverse(j, right)
-            if s + 1 < ITERS:
-                publish(s + 1, j, value)
-            else:
-                for c in range(COMP):
-                    win[s + 1, c, rows, :] = value[c]
-                copy = pltpu.make_async_copy(win.at[s + 1, :, rows], out_hbm.at[:, rows], load_sem.at[j])
-                copy.start()
-                out_copies.append(copy)
+                term = term - plane[a, b].astype(F32) * source[2 * a : 2 * a + 2]
+            terms.append(term)
+        for i in (1, 3, 2):
+            near_copy(s, i, half * 4 + lax.rem(x + i, 4)).wait_recv()
+        for other in range(4):
+            cross_copy(s, other, (1 - half) * 4 + other).wait_recv()
+        plain = jnp.zeros((16, 128), F32)
+        turned = jnp.zeros((16, 128), F32)
+        for i in range(8):
+            block = ibuf[s, lax.rem(q + i, 8)]
+            if i:
+                plain = plain + spectral(2 * i) * block
+            turned = turned + jnp.where(tall_odd, spectral(2 * i + 1), spectral(2 * i - 1)) * block
+        coupled = plain + swap(turned, tall_odd)
+        first = pl.ds(0, 2)
+        value = apply_inverse(first, [terms[b] - coupled[2 * b : 2 * b + 2] for b in range(COMP)])
+        if s + 1 < ITERS:
+            publish_first(s + 1, value)
+        else:
+            for c in range(COMP):
+                out_ref[c, 0:2, :] = value[c]
+
+    @pl.when(half == 0)
+    def _():
+        for j in (1, 2):
+            faces(0, j)
+        for j in range(CHUNKS):
+            instances(0, j, send=False)
+        select(0)
+        halos(0)
+        pl.semaphore_wait(met_sem, len(across))
+        send_across(0)
+        for j in range(CHUNKS):
+            z_copy(0, j).start()
+        finish_first(0)
+        for j in range(CHUNKS):
+            finish(0, j)
+        select(1)
+        for j in (1, 2):
+            faces(1, j)
+        for j in range(CHUNKS):
+            instances(1, j)
+        halos(1)
+        for j in range(CHUNKS):
+            finish(1, j)
+        finish_first(1)
+
+    @pl.when(half == 1)
+    def _():
+        for j in (1, 2):
+            faces(0, j)
+        for j in (0, 1):
+            instances(0, j)
+        select(0)
+        for j in (2, 3):
+            instances(0, j)
+        halos(0)
+        for j in range(CHUNKS):
+            finish(0, j)
+        finish_first(0)
+        for j in (1, 2):
+            faces(1, j)
+        for j in range(CHUNKS):
+            instances(1, j)
+        select(1)
+        halos(1)
+        finish_first(1)
+        for j in range(CHUNKS):
+            finish(1, j)
 
     for i in range(1, 8):
         tab_copy(i, col).wait_send()
@@ -307,11 +427,13 @@
             z_copy(s, j).wait_send()
         for e in (0, 1):
             halo_copy(s, e).wait_send()
+        for other in range(4):
+            cross_copy(s, other, q).wait_send()
+        for i in (1, 2, 3):
+            near_copy(s, i, q).wait_send()
         for i in range(1, 8):
             row_copy(s, i, y).wait_send()
             col_copy(s, i, col).wait_send()
-    for copy in out_copies:
-        copy.wait()
 
 
 def body(objective_grad, face_jacobians, plane_jacobians, diagonal_inverse, neighbours, plane_source):
@@ -328,7 +450,7 @@
         kernel,
         out_shape=jax.ShapeDtypeStruct((COMP, ROWS, 128), F32),
         in_specs=[anywhere] * 5 + [pl.BlockSpec(memory_space=pltpu.SMEM)],
-        out_specs=anywhere,
+        out_specs=pl.BlockSpec(memory_space=pltpu.VMEM),
         scratch_shapes=[
             pltpu.VMEM((COMP, ROWS, 128), F32),
             pltpu.VMEM((FACES, COMP, COMP, ROWS, 128), jnp.bfloat16),
@@ -348,6 +470,7 @@
             pltpu.VMEM((ITERS, 8, 16, 128), F32),
             pltpu.VMEM((ITERS, 8, 16, 128), F32),
             pltpu.VMEM((ITERS, 8, 16, 128), F32),
+            pltpu.VMEM((ITERS, 8, 16, 128), F32),
             pltpu.VMEM((9, 1, 128), jnp.int32),
             dma((5,)),
             dma((ITERS, 4, CHUNKS)), dma((ITERS, 4, CHUNKS)),
@@ -355,7 +478,9 @@
             dma((ITERS, 2)), dma((ITERS, 2)),
             dma((ITERS, 8)), dma((ITERS, 8)),
             dma((ITERS, 8)), dma((ITERS, 8)),
+            dma((ITERS, 8)), dma((ITERS, 8)),
             dma((8,)), dma((8,)),
+            pltpu.SemaphoreType.REGULAR,
         ],
         compiler_params=pltpu.CompilerParams(
             collective_id=0, has_side_effects=True, vmem_limit_bytes=60 * 1024 * 1024

time: 41.2 us -> 39.3 us (0.954)
  Pallas kernels: 38.8 us -> 36.8 us
    pallas_call x1, Pallas kernels: 38.8 us -> 36.8 us  [body(): pl.pallas_call(kernel, out_shape=jax.ShapeDtypeStruct((COMP, ROWS, 128),...]
where the time goes in v3:
time: 39.3 us; the launch traced here: 38.9 us
  Pallas kernels  36.8 us (94%)
  local copies, waits for them, and re-layouts  1.53 us (4%)
  between operations  0.66 us (2%)
    pallas_call x1, Pallas kernels, body(): pl.pallas_call(kernel, out_shape=jax.ShapeDtypeStruct((COMP, ROWS, 128),...  36.8 us
    unnamed x1, local copies, waits for them, and re-layouts  1.53 us

profile of v3, /device:TPU:1, one launch (start us, length us, event | category | flops | bytes accessed | tf_op | source)
XLA Modules:
  0.0 38.9 jit_solution(11978619427991194389)
XLA Ops:
  0.7 36.8 %shard_map.64 = f32[5,32,128]{2,1,0:T(8,128)} custom-call(f32[5,32,128]{2,1,0:T(8,128)} %bitcast.24, bf16[6,5,5,32,128]{4,3,2,1,0:T(8,128)(2,1)} %bitcast.21, bf16[5,5,2,128]{3,2,1,0:T(2,128)(2,1)} %bitcast.25, f32[5,5,32,128]{3,2,1,0:T(8,128)} %bitcast.22, s32[6,2048]{1,0:T(8,128)} %nb_hbm.1, s32[1]{0:T(128)S(6)} %copy.12.src_ref), custom_call_target="tpu_custom_call" | custom-call | tf_op jit(solution)/shard_map/pallas_call | solution.py:449
  37.4 1.5 %copy.13 = f32[2,5,2048]{2,0,1:T(2,128)} copy(f32[2,5,2048]{2,0,1:T(2,128)} %bitcast.23) | data formatting | bytes 163840

commit v4 on v3

--- a/solution.py
+++ b/solution.py
@@ -40,7 +40,7 @@
     grad_hbm, face_hbm, plane_hbm, inv_hbm, nb_hbm, src_ref, out_ref,
     grad, face, plane, inv, nb, lane, side, win, summed, own, xbuf, zsend, zrecv,
     edge, halo, prow, psend, pcol, ibuf, tab,
-    load_sem, xs_sem, xr_sem, zs_sem, zr_sem, hs_sem, hr_sem, as_sem, ar_sem, bs_sem, br_sem, is_sem, ir_sem, ts_sem, tr_sem, met_sem,
+    load_sem, xs_sem, xr_sem, zs_sem, zr_sem, hs_sem, hr_sem, as_sem, ar_sem, bs_sem, br_sem, is_sem, ir_sem, ts_sem, tr_sem, met_sem, mate_sem,
 ):
     q, d = lax.axis_index("inst"), lax.axis_index("space")
     half, x = q // 4, lax.rem(q, 4)
@@ -73,28 +73,79 @@
         other = col_of(i)
         return (q, other // 2 * 16 + y * 2 + lax.rem(other, 2))
 
-    partners = [x_peer(i) for i in (1, 2, 3)] + [before, after]
-    partners += [y_peer(i) for i in range(1, 8)] + [col_peer(i) for i in range(1, 8)]
     across = [((1 - half) * 4 + other, d) for other in range(4)]
+    mate = (q, d + 1 - 2 * core)
     barrier = pltpu.get_barrier_semaphore()
-    for p in partners:
+
+    def greet(p):
         pl.semaphore_signal(barrier, inc=1, device_id=p, device_id_type=MESH)
+
+    def even(p):
+        return (p[0], p[1] - lax.rem(p[1], 2))
+
+    def odd_one(p):
+        return (p[0], p[1] - lax.rem(p[1], 2) + 1)
+
+    for i in (1, 2, 3):
+        greet(even(x_peer(i)))
+
+    @pl.when(core == 1)
+    def _():
+        greet(mate)
 
     @pl.when(half == 0)
     def _():
         for p in across:
-            pl.semaphore_signal(barrier, inc=1, device_id=p, device_id_type=MESH)
-
-    def enter():
-        @pl.when(half == 0)
+            greet(even(p))
+
+    greet(odd_one(after))
+    for i in range(1, 8):
+        greet(odd_one(y_peer(i)))
+    for i in range(2, 7):
+        greet(odd_one(col_peer(i)))
+
+    @pl.when(core == 0)
+    def _():
+        greet(odd_one(before))
+        greet(odd_one(col_peer(1)))
+        greet(odd_one(col_peer(7)))
+
+    @pl.when(core == 1)
+    def _():
+        greet(odd_one(col_peer(1)))
+
+    def tell_mate():
+        pl.semaphore_signal(mate_sem, inc=1, device_id=mate, device_id_type=MESH)
+
+    def enter_inst():
+        @pl.when(core == 0)
         def _():
-            pl.semaphore_wait(barrier, len(partners))
-
-        @pl.when(half == 1)
+            @pl.when(half == 0)
+            def _():
+                pl.semaphore_wait(barrier, 7)
+
+            @pl.when(half == 1)
+            def _():
+                pl.semaphore_wait(barrier, 15)
+                for p in across:
+                    pl.semaphore_signal(met_sem, inc=1, device_id=p, device_id_type=MESH)
+                    pl.semaphore_signal(met_sem, inc=1, device_id=(p[0], p[1] + 1), device_id_type=MESH)
+
+            tell_mate()
+
+        @pl.when(core == 1)
         def _():
-            pl.semaphore_wait(barrier, len(partners) + len(across))
-            for p in across:
-                pl.semaphore_signal(met_sem, inc=1, device_id=p, device_id_type=MESH)
+            pl.semaphore_wait(mate_sem, 1)
+
+    def enter_space():
+        @pl.when(core == 1)
+        def _():
+            pl.semaphore_wait(barrier, 30)
+            tell_mate()
+
+        @pl.when(core == 0)
+        def _():
+            pl.semaphore_wait(mate_sem, 1)
 
     def x_copy(s, i, j):
         rows = pl.ds(8 * j, 8)
@@ -195,15 +246,18 @@
         for c in range(COMP):
             win[s, c, TOP : TOP + 2, :] = value[c]
             edge[s, 0, 2 * c : 2 * c + 2, :] = value[c]
-        if s == 0:
-            enter()
-        send_first(s, s == 0)
-        for i in (4, 3, 5, 2, 6, 1, 7):
-            row_copy(s, i, y).start()
-        halo_copy(s, 0).start()
+        if s:
+            send_first(s, False)
+            send_space(s, 0)
         block = edge[s, 0]
         ibuf[s, q] = block
         prow[s, y] = block
+
+    def send_space(s, e):
+        if e == 0:
+            for i in (4, 3, 5, 2, 6, 1, 7):
+                row_copy(s, i, y).start()
+        halo_copy(s, e).start()
 
     def publish(s, j, value):
         for c in range(COMP):
@@ -217,7 +271,8 @@
         if j == CHUNKS - 1:
             for c in range(COMP):
                 edge[s, 1, 2 * c : 2 * c + 2, :] = value[c][6:8]
-            halo_copy(s, 1).start()
+            if s:
+                send_space(s, 1)
 
     def apply_inverse(rows, values):
         out = []
@@ -274,16 +329,21 @@
 
     tab[8] = jnp.full((1, 128), src_ref[0], jnp.int32)
     tab[col] = jnp.full((1, 128), src_ref[0], jnp.int32)
+    enter_inst()
     loads[0].wait()
     loads[1].wait()
     for j in range(CHUNKS):
         value = apply_inverse(pl.ds(8 * j, 8), [grad[b, pl.ds(8 * j, 8), :] for b in range(COMP)])
         if j == 0:
             publish_first(0, [v[0:2] for v in value])
-            for i in range(1, 8):
-                tab_copy(i, col).start()
+            send_first(0, True)
         publish(0, j, value)
 
+    enter_space()
+    send_space(0, 0)
+    send_space(0, 1)
+    for i in range(1, 8):
+        tab_copy(i, col).start()
     loads[2].wait()
     for k in range(FACES):
         for block in range(ROWS // 2):
@@ -385,25 +445,23 @@
         finish_first(0)
         for j in range(CHUNKS):
             finish(0, j)
-        select(1)
         for j in (1, 2):
             faces(1, j)
+        select(1)
         for j in range(CHUNKS):
             instances(1, j)
         halos(1)
+        finish_first(1)
         for j in range(CHUNKS):
             finish(1, j)
-        finish_first(1)
 
     @pl.when(half == 1)
     def _():
         for j in (1, 2):
             faces(0, j)
-        for j in (0, 1):
+        for j in range(CHUNKS):
             instances(0, j)
         select(0)
-        for j in (2, 3):
-            instances(0, j)
         halos(0)
         for j in range(CHUNKS):
             finish(0, j)
@@ -481,6 +539,7 @@
             dma((ITERS, 8)), dma((ITERS, 8)),
             dma((8,)), dma((8,)),
             pltpu.SemaphoreType.REGULAR,
+            pltpu.SemaphoreType.REGULAR,
         ],
         compiler_params=pltpu.CompilerParams(
             collective_id=0, has_side_effects=True, vmem_limit_bytes=60 * 1024 * 1024

time: 39.3 us -> 38.3 us (0.975)
  the two profiles are of different devices: /device:TPU:1 before, /device:TPU:8 now
where the time goes in v4:
time: 38.3 us; the launch traced here: 38.2 us
  Pallas kernels  36 us (94%)
  local copies, waits for them, and re-layouts  1.53 us (4%)
  between operations  0.66 us (2%)
    pallas_call x1, Pallas kernels, body(): pl.pallas_call(kernel, out_shape=jax.ShapeDtypeStruct((COMP, ROWS, 128),...  36 us
    unnamed x1, local copies, waits for them, and re-layouts  1.53 us

profile of v4, /device:TPU:8, one launch (start us, length us, event | category | flops | bytes accessed | tf_op | source)
XLA Modules:
  0.0 38.2 jit_solution(18098608962163997137)
XLA Ops:
  0.7 36.0 %shard_map.64 = f32[5,32,128]{2,1,0:T(8,128)} custom-call(f32[5,32,128]{2,1,0:T(8,128)} %bitcast.24, bf16[6,5,5,32,128]{4,3,2,1,0:T(8,128)(2,1)} %bitcast.21, bf16[5,5,2,128]{3,2,1,0:T(2,128)(2,1)} %bitcast.25, f32[5,5,32,128]{3,2,1,0:T(8,128)} %bitcast.22, s32[6,2048]{1,0:T(8,128)} %nb_hbm.1, s32[1]{0:T(128)S(6)} %copy.12.src_ref), custom_call_target="tpu_custom_call" | custom-call | tf_op jit(solution)/shard_map/pallas_call | solution.py:507
  36.6 1.5 %copy.13 = f32[2,5,2048]{2,0,1:T(2,128)} copy(f32[2,5,2048]{2,0,1:T(2,128)} %bitcast.23) | data formatting | bytes 163840

commit v5 on v4

--- a/solution.py
+++ b/solution.py
@@ -39,8 +39,8 @@
 def kernel(
     grad_hbm, face_hbm, plane_hbm, inv_hbm, nb_hbm, src_ref, out_ref,
     grad, face, plane, inv, nb, lane, side, win, summed, own, xbuf, zsend, zrecv,
-    edge, halo, prow, psend, pcol, ibuf, tab,
-    load_sem, xs_sem, xr_sem, zs_sem, zr_sem, hs_sem, hr_sem, as_sem, ar_sem, bs_sem, br_sem, is_sem, ir_sem, ts_sem, tr_sem, met_sem, mate_sem,
+    edge, halo, prow, psend, pcol, ibuf, zfirst, zgot, tab,
+    load_sem, xs_sem, xr_sem, zs_sem, zr_sem, hs_sem, hr_sem, as_sem, ar_sem, bs_sem, br_sem, is_sem, ir_sem, ts_sem, tr_sem, met_sem, mate_sem, fs_sem, fr_sem,
 ):
     q, d = lax.axis_index("inst"), lax.axis_index("space")
     half, x = q // 4, lax.rem(q, 4)
@@ -127,9 +127,8 @@
             @pl.when(half == 1)
             def _():
                 pl.semaphore_wait(barrier, 15)
-                for p in across:
-                    pl.semaphore_signal(met_sem, inc=1, device_id=p, device_id_type=MESH)
-                    pl.semaphore_signal(met_sem, inc=1, device_id=(p[0], p[1] + 1), device_id_type=MESH)
+                pl.semaphore_signal(met_sem, inc=1, device_id=z_peer, device_id_type=MESH)
+                pl.semaphore_signal(met_sem, inc=1, device_id=(z_peer[0], d + 1), device_id_type=MESH)
 
             tell_mate()
 
@@ -182,21 +181,21 @@
         return pltpu.make_async_remote_copy(
             src_ref=edge.at[s, 0], dst_ref=prow.at[s, slot],
             send_sem=as_sem.at[s, i], recv_sem=ar_sem.at[s, slot],
-            device_id=y_peer(i), device_id_type=MESH,
+            device_id=col_peer(i), device_id_type=MESH,
         )
 
     def col_copy(s, i, slot):
         return pltpu.make_async_remote_copy(
             src_ref=psend.at[s, i], dst_ref=pcol.at[s, slot],
             send_sem=bs_sem.at[s, i], recv_sem=br_sem.at[s, slot],
-            device_id=col_peer(i), device_id_type=MESH,
+            device_id=y_peer(i), device_id_type=MESH,
         )
 
     def tab_copy(i, slot):
         return pltpu.make_async_remote_copy(
             src_ref=tab.at[8], dst_ref=tab.at[slot],
             send_sem=ts_sem.at[i], recv_sem=tr_sem.at[slot],
-            device_id=col_peer(i), device_id_type=MESH,
+            device_id=y_peer(i), device_id_type=MESH,
         )
 
     odd = lax.rem(lax.broadcasted_iota(jnp.int32, (8, 128), 0), 2) == 1
@@ -211,8 +210,6 @@
             )
         coef.append((straight, crossed))
 
-    tall_odd = lax.rem(lax.broadcasted_iota(jnp.int32, (16, 128), 0), 2) == 1
-
     def swap(v, mask):
         return jnp.where(mask, pltpu.roll(v, 1, 0), pltpu.roll(v, v.shape[0] - 1, 0))
 
@@ -234,29 +231,51 @@
         for other in range(4):
             cross_copy(s, other, q).start()
 
-    def send_first(s, held):
-        if held:
-            pl.when(half == 1)(lambda: send_across(s))
-        else:
-            send_across(s)
+    def send_first(s):
+        pl.when(half == 1)(lambda: send_across(s))
         for i in (2, 1, 3):
             near_copy(s, i, q).start()
+
+    def first_copy(s):
+        return pltpu.make_async_remote_copy(
+            src_ref=zfirst.at[s], dst_ref=zgot.at[s], send_sem=fs_sem.at[s], recv_sem=fr_sem.at[s],
+            device_id=z_peer, device_id_type=MESH,
+        )
+
+    def first_sum(s, kind, group, h):
+        straight, crossed = coef[kind]
+        rows = pl.ds(8 * h, 8)
+        values = [ibuf[s, 4 * group + other, rows, :] for other in range(4)]
+        plain, turned = straight[0] * values[0], crossed[0] * values[0]
+        for other in range(1, 4):
+            plain = plain + straight[other] * values[other]
+            turned = turned + crossed[other] * values[other]
+        return plain + swap(turned, odd)
+
+    def near_arrivals(s):
+        for i in (1, 3, 2):
+            near_copy(s, i, half * 4 + lax.rem(x + i, 4)).wait_recv()
+
+    def first_across(s):
+        near_arrivals(s)
+        for h in (0, 1):
+            zfirst[s, 8 * h : 8 * h + 8, :] = first_sum(s, 1, 0, h)
 
     def publish_first(s, value):
         for c in range(COMP):
             win[s, c, TOP : TOP + 2, :] = value[c]
             edge[s, 0, 2 * c : 2 * c + 2, :] = value[c]
         if s:
-            send_first(s, False)
+            send_first(s)
             send_space(s, 0)
         block = edge[s, 0]
         ibuf[s, q] = block
-        prow[s, y] = block
+        prow[s, col] = block
 
     def send_space(s, e):
         if e == 0:
             for i in (4, 3, 5, 2, 6, 1, 7):
-                row_copy(s, i, y).start()
+                row_copy(s, i, col).start()
         halo_copy(s, e).start()
 
     def publish(s, j, value):
@@ -328,7 +347,7 @@
             z_copy(s, j).start()
 
     tab[8] = jnp.full((1, 128), src_ref[0], jnp.int32)
-    tab[col] = jnp.full((1, 128), src_ref[0], jnp.int32)
+    tab[y] = jnp.full((1, 128), src_ref[0], jnp.int32)
     enter_inst()
     loads[0].wait()
     loads[1].wait()
@@ -336,14 +355,14 @@
         value = apply_inverse(pl.ds(8 * j, 8), [grad[b, pl.ds(8 * j, 8), :] for b in range(COMP)])
         if j == 0:
             publish_first(0, [v[0:2] for v in value])
-            send_first(0, True)
+            send_first(0)
         publish(0, j, value)
 
     enter_space()
     send_space(0, 0)
     send_space(0, 1)
     for i in range(1, 8):
-        tab_copy(i, col).start()
+        tab_copy(i, y).start()
     loads[2].wait()
     for k in range(FACES):
         for block in range(ROWS // 2):
@@ -355,21 +374,22 @@
 
     def select(s):
         for i in range(1, 8):
-            row_copy(s, i, lax.rem(y + i, 8)).wait_recv()
+            row_copy(s, i, col_of(i)).wait_recv()
         if s == 0:
             for i in range(1, 8):
-                tab_copy(i, col_of(i)).wait_recv()
+                tab_copy(i, lax.rem(y + i, 8)).wait_recv()
         blocks = [prow[s, r] for r in range(8)]
         for i in (4, 3, 5, 2, 6, 1, 7, 0):
-            want = jnp.broadcast_to((tab[col_of(i)] >> 1) & 7, (16, 128))
+            wanted = tab[lax.rem(y + i, 8)]
+            want = jnp.broadcast_to((wanted >> 4) * 2 + (wanted & 1), (16, 128))
             chosen = blocks[7]
             for r in range(7):
                 chosen = jnp.where(want == r, blocks[r], chosen)
             if i == 0:
-                pcol[s, col] = chosen
+                pcol[s, y] = chosen
             else:
                 psend[s, i] = chosen
-                col_copy(s, i, col).start()
+                col_copy(s, i, y).start()
 
     def halos(s):
         for e in (0, 1):
@@ -396,11 +416,11 @@
                 else:
                     out_ref[c, rows, :] = value[c]
 
-    def finish_first(s):
+    def finish_first(s, upper):
         for i in range(1, 8):
-            col_copy(s, i, col_of(i)).wait_recv()
+            col_copy(s, i, lax.rem(y + i, 8)).wait_recv()
         mine = tab[8]
-        want = jnp.broadcast_to((mine >> 4) * 2 + (mine & 1), (16, 128))
+        want = jnp.broadcast_to((mine >> 1) & 7, (16, 128))
         source = pcol[s, 7]
         for r in range(7):
             source = jnp.where(want == r, pcol[s, r], source)
@@ -410,20 +430,17 @@
             for a in range(COMP):
                 term = term - plane[a, b].astype(F32) * source[2 * a : 2 * a + 2]
             terms.append(term)
-        for i in (1, 3, 2):
-            near_copy(s, i, half * 4 + lax.rem(x + i, 4)).wait_recv()
-        for other in range(4):
-            cross_copy(s, other, (1 - half) * 4 + other).wait_recv()
-        plain = jnp.zeros((16, 128), F32)
-        turned = jnp.zeros((16, 128), F32)
-        for i in range(8):
-            block = ibuf[s, lax.rem(q + i, 8)]
-            if i:
-                plain = plain + spectral(2 * i) * block
-            turned = turned + jnp.where(tall_odd, spectral(2 * i + 1), spectral(2 * i - 1)) * block
-        coupled = plain + swap(turned, tall_odd)
+        if upper:
+            near_arrivals(s)
+            first_copy(s).wait_recv()
+            coupled = [first_sum(s, 0, 1, h) + zgot[s, 8 * h : 8 * h + 8, :] for h in (0, 1)]
+        else:
+            for other in range(4):
+                cross_copy(s, other, (1 - half) * 4 + other).wait_recv()
+            coupled = [first_sum(s, 0, 0, h) + first_sum(s, 1, 1, h) for h in (0, 1)]
+        coupled = [coupled[b // 4][2 * b % 8 : 2 * b % 8 + 2] for b in range(COMP)]
         first = pl.ds(0, 2)
-        value = apply_inverse(first, [terms[b] - coupled[2 * b : 2 * b + 2] for b in range(COMP)])
+        value = apply_inverse(first, [terms[b] - coupled[b] for b in range(COMP)])
         if s + 1 < ITERS:
             publish_first(s + 1, value)
         else:
@@ -438,20 +455,23 @@
             instances(0, j, send=False)
         select(0)
         halos(0)
-        pl.semaphore_wait(met_sem, len(across))
-        send_across(0)
+        first_across(0)
+        pl.semaphore_wait(met_sem, 1)
+        first_copy(0).start()
         for j in range(CHUNKS):
             z_copy(0, j).start()
-        finish_first(0)
+        finish_first(0, False)
         for j in range(CHUNKS):
             finish(0, j)
         for j in (1, 2):
             faces(1, j)
         select(1)
+        first_across(1)
+        first_copy(1).start()
         for j in range(CHUNKS):
             instances(1, j)
         halos(1)
-        finish_first(1)
+        finish_first(1, False)
         for j in range(CHUNKS):
             finish(1, j)
 
@@ -465,19 +485,19 @@
         halos(0)
         for j in range(CHUNKS):
             finish(0, j)
-        finish_first(0)
+        finish_first(0, True)
         for j in (1, 2):
             faces(1, j)
         for j in range(CHUNKS):
             instances(1, j)
         select(1)
         halos(1)
-        finish_first(1)
+        finish_first(1, True)
         for j in range(CHUNKS):
             finish(1, j)
 
     for i in range(1, 8):
-        tab_copy(i, col).wait_send()
+        tab_copy(i, y).wait_send()
     for s in range(ITERS):
         for j in range(CHUNKS):
             for i in (1, 2, 3):
@@ -485,13 +505,21 @@
             z_copy(s, j).wait_send()
         for e in (0, 1):
             halo_copy(s, e).wait_send()
-        for other in range(4):
-            cross_copy(s, other, q).wait_send()
+
+        @pl.when(half == 0)
+        def _():
+            first_copy(s).wait_send()
+
+        @pl.when(half == 1)
+        def _():
+            for other in range(4):
+                cross_copy(s, other, q).wait_send()
+
         for i in (1, 2, 3):
             near_copy(s, i, q).wait_send()
         for i in range(1, 8):
-            row_copy(s, i, y).wait_send()
-            col_copy(s, i, col).wait_send()
+            row_copy(s, i, col).wait_send()
+            col_copy(s, i, y).wait_send()
 
 
 def body(objective_grad, face_jacobians, plane_jacobians, diagonal_inverse, neighbours, plane_source):
@@ -529,6 +557,8 @@
             pltpu.VMEM((ITERS, 8, 16, 128), F32),
             pltpu.VMEM((ITERS, 8, 16, 128), F32),
             pltpu.VMEM((ITERS, 8, 16, 128), F32),
+            pltpu.VMEM((ITERS, 16, 128), F32),
+            pltpu.VMEM((ITERS, 16, 128), F32),
             pltpu.VMEM((9, 1, 128), jnp.int32),
             dma((5,)),
             dma((ITERS, 4, CHUNKS)), dma((ITERS, 4, CHUNKS)),
@@ -540,6 +570,7 @@
             dma((8,)), dma((8,)),
             pltpu.SemaphoreType.REGULAR,
             pltpu.SemaphoreType.REGULAR,
+            dma((ITERS,)), dma((ITERS,)),
         ],
         compiler_params=pltpu.CompilerParams(
             collective_id=0, has_side_effects=True, vmem_limit_bytes=60 * 1024 * 1024

time: 38.3 us -> 37.1 us (0.969)
  the two profiles are of different devices: /device:TPU:8 before, /device:TPU:64 now
where the time goes in v5:
time: 37.1 us; the launch traced here: 37 us
  Pallas kernels  34.8 us (94%)
  local copies, waits for them, and re-layouts  1.53 us (4%)
  between operations  0.66 us (2%)
    pallas_call x1, Pallas kernels, body(): pl.pallas_call(kernel, out_shape=jax.ShapeDtypeStruct((COMP, ROWS, 128),...  34.8 us
    unnamed x1, local copies, waits for them, and re-layouts  1.53 us

profile of v5, /device:TPU:64, one launch (start us, length us, event | category | flops | bytes accessed | tf_op | source)
XLA Modules:
  0.0 37.0 jit_solution(12184656393997844110)
XLA Ops:
  0.7 34.8 %shard_map.64 = f32[5,32,128]{2,1,0:T(8,128)} custom-call(f32[5,32,128]{2,1,0:T(8,128)} %bitcast.24, bf16[6,5,5,32,128]{4,3,2,1,0:T(8,128)(2,1)} %bitcast.21, bf16[5,5,2,128]{3,2,1,0:T(2,128)(2,1)} %bitcast.25, f32[5,5,32,128]{3,2,1,0:T(8,128)} %bitcast.22, s32[6,2048]{1,0:T(8,128)} %nb_hbm.1, s32[1]{0:T(128)S(6)} %copy.12.src_ref), custom_call_target="tpu_custom_call" | custom-call | tf_op jit(solution)/shard_map/pallas_call | solution.py:535
  35.4 1.5 %copy.13 = f32[2,5,2048]{2,0,1:T(2,128)} copy(f32[2,5,2048]{2,0,1:T(2,128)} %bitcast.23) | data formatting | bytes 163840

commit v6 on v5

--- a/solution.py
+++ b/solution.py
@@ -447,19 +447,45 @@
             for c in range(COMP):
                 out_ref[c, 0:2, :] = value[c]
 
+    def drain(s):
+        if s == 0:
+            for i in range(1, 8):
+                tab_copy(i, y).wait_send()
+        for j in range(CHUNKS):
+            for i in (1, 2, 3):
+                x_copy(s, i, j).wait_send()
+            z_copy(s, j).wait_send()
+        for e in (0, 1):
+            halo_copy(s, e).wait_send()
+
+        @pl.when(half == 0)
+        def _():
+            first_copy(s).wait_send()
+
+        @pl.when(half == 1)
+        def _():
+            for other in range(4):
+                cross_copy(s, other, q).wait_send()
+
+        for i in (1, 2, 3):
+            near_copy(s, i, q).wait_send()
+        for i in range(1, 8):
+            row_copy(s, i, col).wait_send()
+            col_copy(s, i, y).wait_send()
+
     @pl.when(half == 0)
     def _():
         for j in (1, 2):
             faces(0, j)
+        select(0)
         for j in range(CHUNKS):
             instances(0, j, send=False)
-        select(0)
-        halos(0)
         first_across(0)
         pl.semaphore_wait(met_sem, 1)
         first_copy(0).start()
         for j in range(CHUNKS):
             z_copy(0, j).start()
+        halos(0)
         finish_first(0, False)
         for j in range(CHUNKS):
             finish(0, j)
@@ -470,7 +496,9 @@
         first_copy(1).start()
         for j in range(CHUNKS):
             instances(1, j)
+        drain(0)
         halos(1)
+        drain(1)
         finish_first(1, False)
         for j in range(CHUNKS):
             finish(1, j)
@@ -479,9 +507,11 @@
     def _():
         for j in (1, 2):
             faces(0, j)
-        for j in range(CHUNKS):
+        for j in (0, 1):
             instances(0, j)
         select(0)
+        for j in (2, 3):
+            instances(0, j)
         halos(0)
         for j in range(CHUNKS):
             finish(0, j)
@@ -490,36 +520,13 @@
             faces(1, j)
         for j in range(CHUNKS):
             instances(1, j)
+        drain(0)
         select(1)
         halos(1)
+        drain(1)
         finish_first(1, True)
         for j in range(CHUNKS):
             finish(1, j)
-
-    for i in range(1, 8):
-        tab_copy(i, y).wait_send()
-    for s in range(ITERS):
-        for j in range(CHUNKS):
-            for i in (1, 2, 3):
-                x_copy(s, i, j).wait_send()
-            z_copy(s, j).wait_send()
-        for e in (0, 1):
-            halo_copy(s, e).wait_send()
-
-        @pl.when(half == 0)
-        def _():
-            first_copy(s).wait_send()
-
-        @pl.when(half == 1)
-        def _():
-            for other in range(4):
-                cross_copy(s, other, q).wait_send()
-
-        for i in (1, 2, 3):
-            near_copy(s, i, q).wait_send()
-        for i in range(1, 8):
-            row_copy(s, i, col).wait_send()
-            col_copy(s, i, y).wait_send()
 
 
 def body(objective_grad, face_jacobians, plane_jacobians, diagonal_inverse, neighbours, plane_source):

time: 37.1 us -> 36.5 us (0.984)
  the two profiles are of different devices: /device:TPU:64 before, /device:TPU:8 now
where the time goes in v6:
time: 36.5 us; the launch traced here: 36.3 us
  Pallas kernels  34.1 us (93%)
  local copies, waits for them, and re-layouts  1.53 us (4%)
  between operations  0.66 us (2%)
    pallas_call x1, Pallas kernels, body(): pl.pallas_call(kernel, out_shape=jax.ShapeDtypeStruct((COMP, ROWS, 128),...  34.1 us
    unnamed x1, local copies, waits for them, and re-layouts  1.53 us

profile of v6, /device:TPU:8, one launch (start us, length us, event | category | flops | bytes accessed | tf_op | source)
XLA Modules:
  0.0 36.3 jit_solution(3963303388560614150)
XLA Ops:
  0.7 34.1 %shard_map.64 = f32[5,32,128]{2,1,0:T(8,128)} custom-call(f32[5,32,128]{2,1,0:T(8,128)} %bitcast.24, bf16[6,5,5,32,128]{4,3,2,1,0:T(8,128)(2,1)} %bitcast.21, bf16[5,5,2,128]{3,2,1,0:T(2,128)(2,1)} %bitcast.25, f32[5,5,32,128]{3,2,1,0:T(8,128)} %bitcast.22, s32[6,2048]{1,0:T(8,128)} %nb_hbm.1, s32[1]{0:T(128)S(6)} %copy.12.src_ref), custom_call_target="tpu_custom_call" | custom-call | tf_op jit(solution)/shard_map/pallas_call | solution.py:542
  34.8 1.5 %copy.13 = f32[2,5,2048]{2,0,1:T(2,128)} copy(f32[2,5,2048]{2,0,1:T(2,128)} %bitcast.23) | data formatting | bytes 163840

commit v7 on v6

--- a/solution.py
+++ b/solution.py
@@ -356,10 +356,11 @@
         if j == 0:
             publish_first(0, [v[0:2] for v in value])
             send_first(0)
+        if j == 0:
+            enter_space()
+            send_space(0, 0)
         publish(0, j, value)
 
-    enter_space()
-    send_space(0, 0)
     send_space(0, 1)
     for i in range(1, 8):
         tab_copy(i, y).start()

time: 36.5 us -> 35.7 us (0.978)
  the two profiles are of different devices: /device:TPU:8 before, /device:TPU:2 now
where the time goes in v7:
time: 35.7 us; the launch traced here: 35.6 us
  Pallas kernels  33.4 us (94%)
  local copies, waits for them, and re-layouts  1.53 us (4%)
  between operations  0.66 us (2%)
    pallas_call x1, Pallas kernels, body(): pl.pallas_call(kernel, out_shape=jax.ShapeDtypeStruct((COMP, ROWS, 128),...  33.4 us
    unnamed x1, local copies, waits for them, and re-layouts  1.53 us

profile of v7, /device:TPU:2, one launch (start us, length us, event | category | flops | bytes accessed | tf_op | source)
XLA Modules:
  0.0 35.6 jit_solution(348537536510830016)
XLA Ops:
  0.7 33.4 %shard_map.64 = f32[5,32,128]{2,1,0:T(8,128)} custom-call(f32[5,32,128]{2,1,0:T(8,128)} %bitcast.24, bf16[6,5,5,32,128]{4,3,2,1,0:T(8,128)(2,1)} %bitcast.21, bf16[5,5,2,128]{3,2,1,0:T(2,128)(2,1)} %bitcast.25, f32[5,5,32,128]{3,2,1,0:T(8,128)} %bitcast.22, s32[6,2048]{1,0:T(8,128)} %nb_hbm.1, s32[1]{0:T(128)S(6)} %copy.12.src_ref), custom_call_target="tpu_custom_call" | custom-call | tf_op jit(solution)/shard_map/pallas_call | solution.py:543
  34.0 1.5 %copy.13 = f32[2,5,2048]{2,0,1:T(2,128)} copy(f32[2,5,2048]{2,0,1:T(2,128)} %bitcast.23) | data formatting | bytes 163840
